TPU v7x, 32 devices: a whole 2x2x4 slice. The times are simulated.
32 devices in a mesh: parts: 2 (over x), leaf: 16 (over z, y, core).
Axes of the slice: x: 2, y: 2, z: 4, core: 2. Of those that a mesh axis runs over, the one named last changes fastest.
Arguments:
- points: float32 [3, 65536], P(None, ('parts', 'leaf')), parts along dimension 1, may hold values from 0 to 18
- charges: bfloat16 [16, 65536], P(None, ('parts', 'leaf')), parts along dimension 1, may hold values from -6 to 6
- near_list: int32 [256, 12], P(('parts', 'leaf')), parts along dimension 0, may hold values from -1 to 127, as said below
- basis: bfloat16 [256, 64, 256], P(('parts', 'leaf')), parts along dimension 0, may hold values from -0.75 to 0.75
- leaf_transfer: bfloat16 [256, 64, 64], P(('parts', 'leaf')), parts along dimension 0, may hold values from -0.25 to 0.25
- cluster_transfer: bfloat16 [32, 64, 64], P(('parts', 'leaf')), parts along dimension 0, may hold values from -0.25 to 0.25
- couple_one: bfloat16 [32, 6, 64, 64], P(('parts', 'leaf')), parts along dimension 0, may hold values from -0.3125 to 0.3125
- far_list: int32 [32, 6], P(('parts', 'leaf')), parts along dimension 0, may hold values from -1 to 15, as said below
- couple_two: bfloat16 [4, 2, 64, 64], P('parts'), parts along dimension 0, may hold values from -0.5 to 0.5
Outputs:
- potential: float32 [16, 65536], P(None, ('parts', 'leaf')), parts along dimension 1
There are 2 independent parts, one for each index of `parts`. A program takes and returns all parts, laid end to end along the dimension named above; each array names one. Nothing has to cross between parts.
Inputs may be any that keep to these rules, and one draw needn't show every extreme that they name: `near_list`: row i holds distinct leaves j with |j - i| <= 8, the used entries first and -1 after them; every row has at least one used entry; some row is full. `far_list`: slot s of row c holds -1 or c plus the s-th of the offsets -4 to -2 and 2 to 4 in increasing order.
All inputs are finite; a program needn't handle non-finite values.
Results may differ from a plain program's by a relative error of at most 0.0029.
Values may be sent and summed in bfloat16 or wider, within the bound.
A program may use at most 64 MiB of HBM per device.

v0:
```python
import math

import jax
import jax.numpy as jnp
from jax import lax
from jax.sharding import PartitionSpec as P

FAR_REACH = 4


inv_four_pi = 1.0 / (4.0 * math.pi)
soften = 0.01


def padded(cells, sides, width):
    for axis, dim in sides:
        count = lax.axis_size(axis)
        ends = count - 1
        head = lax.slice_in_dim(cells, 0, width, axis=dim)
        tail = lax.slice_in_dim(cells, cells.shape[dim] - width, cells.shape[dim], axis=dim)
        cells = jnp.concatenate(
            [
                lax.ppermute(tail, axis, [(i, (i + 1) % count) for i in range(ends)]),
                cells,
                lax.ppermute(head, axis, [((i + 1) % count, i) for i in range(ends)]),
            ],
            axis=dim,
        )
    return cells


def passed_along(value, axis, steps):
    count = lax.axis_size(axis)
    first, last = (max(0, -steps), min(count, count - steps))
    return lax.ppermute(value, axis, [(source, source + steps) for source in range(first, last)])


def near_kernel(target, source, usable):
    square = jnp.square(target[0][None, :, None] - source[0][:, None, :])
    square = square + jnp.square(target[1][None, :, None] - source[1][:, None, :])
    square = square + jnp.square(target[2][None, :, None] - source[2][:, None, :])
    return usable[:, None, None] * inv_four_pi / jnp.sqrt(square + soften)


def shards(
    points,
    charges,
    near_list,
    basis,
    leaf_transfer,
    cluster_transfer,
    couple_one,
    far_list,
    couple_two,
):
    high = lax.Precision.HIGHEST
    leaf_count = basis.shape[0]
    leaf_width = basis.shape[2]
    vector_count = charges.shape[0]
    rank_size = basis.shape[1]
    device = lax.axis_index("leaf")
    rim_width = leaf_count * leaf_width
    wide_points = padded(points, (("leaf", 1),), rim_width)
    wide_charges = padded(charges, (("leaf", 1),), rim_width)
    grid_points = wide_points.reshape(3, 3 * leaf_count, leaf_width)
    grid_charges = wide_charges.reshape(vector_count, 3 * leaf_count, leaf_width)
    own_points = points.reshape(3, leaf_count, leaf_width)
    first_leaf = (device - 1) * leaf_count
    usable = (near_list >= 0).astype(jnp.float32)
    local_index = jnp.where(near_list >= 0, near_list - first_leaf, 0)

    def one_leaf(packed):
        target, index, valid = packed
        source = grid_points[:, index, :]
        source_charge = grid_charges[:, index, :]
        kernel = near_kernel(target, source, valid).astype(jnp.bfloat16)
        return jnp.einsum("npq,vnq->vp", kernel, source_charge, preferred_element_type=jnp.float32)

    near = lax.map(one_leaf, (jnp.moveaxis(own_points, 1, 0), local_index, usable))
    near = jnp.moveaxis(near, 0, 1).reshape(vector_count, leaf_count * leaf_width)
    own_charges = charges.reshape(vector_count, leaf_count, leaf_width)
    leaf_moment = jnp.einsum("lrp,vlp->lrv", basis, own_charges, preferred_element_type=jnp.float32)
    transfer = leaf_transfer.astype(jnp.float32)
    moment_one = jnp.einsum("kab,kbv->av", transfer, leaf_moment, precision=high)
    upper = cluster_transfer[0].astype(jnp.float32)
    own_term = jnp.dot(upper, moment_one, precision=high)
    group_count = couple_two.shape[0]
    group_size = lax.axis_size("leaf") // group_count
    own_group = device // group_size
    every_term = lax.all_gather(own_term[None], "leaf", axis=0, tiled=True)
    moment_two = every_term.reshape(group_count, group_size, rank_size, vector_count).sum(axis=1)
    coupling_row = couple_two[own_group].astype(jnp.float32)
    mask_row = (jnp.arange(group_count) != own_group).astype(jnp.float32)
    local_two = jnp.einsum("hab,h,hbv->av", coupling_row, mask_row, moment_two, precision=high)
    offsets = list(range(-FAR_REACH, -1)) + list(range(2, FAR_REACH + 1))
    local_one = jnp.einsum("ba,bv->av", upper, local_two, precision=high)
    for slot, offset in enumerate(offsets):
        arrived = passed_along(moment_one[None], "leaf", -offset)
        valid = (far_list[0, slot] >= 0).astype(jnp.float32)
        local_one = local_one + jnp.dot(
            couple_one[0, slot].astype(jnp.float32), arrived[0] * valid, precision=high
        )
    local_leaf = jnp.einsum("kba,bv->kav", transfer, local_one, precision=high).astype(jnp.bfloat16)
    far = jnp.einsum("krv,krp->vkp", local_leaf, basis, preferred_element_type=jnp.float32)
    return near + far.reshape(vector_count, leaf_count * leaf_width)


def solution(mesh):
    return jax.shard_map(
        shards,
        mesh=mesh,
        in_specs=(
            P(None, ("parts", "leaf")),
            P(None, ("parts", "leaf")),
            P(("parts", "leaf"), None),
            P(("parts", "leaf"), None, None),
            P(("parts", "leaf"), None, None),
            P(("parts", "leaf"), None, None),
            P(("parts", "leaf"), None, None, None),
            P(("parts", "leaf"), None),
            P("parts", None, None, None),
        ),
        out_specs=P(None, ("parts", "leaf")),
        check_vma=False,
    )
```

profile of v0, /device:TPU:1, one launch (start us, length us, event | category | flops | bytes accessed | tf_op | source)
XLA Modules:
  0.0 89.8 jit_solution(17489175424012895810)
XLA Ops:
  0.0 2.1 %collective-permute-start.1 = (bf16[16,2048]{1,0:T(8,128)(2,1)}, bf16[16,2048]{1,0:T(8,128)(2,1)S(1)}, u32[]{:S(2)}, u32[]{:S(2)}) collective-permute-start(bf16[16,2048]{1,0:T(8,128)(2,1)} %param.12), channel_id=1, source_target_pairs={{1,0},{2,1},{3,2},{4,3},{5,4},{6,5},{7,6},{8,7},{9,8},{10,9},{11,1... | collective-permute-start | bytes 196616 | tf_op jit(solution)/shard_map/ppermute | solution.py:25
  2.1 4.5 %collective-permute-start = (bf16[16,2048]{1,0:T(8,128)(2,1)}, bf16[16,2048]{1,0:T(8,128)(2,1)S(1)}, u32[]{:S(2)}, u32[]{:S(2)}) collective-permute-start(bf16[16,2048]{1,0:T(8,128)(2,1)} %param.12), channel_id=1, source_target_pairs={{0,1},{1,2},{2,3},{3,4},{4,5},{5,6},{6,7},{7,8},{8,9},{9,10},{10,1... | collective-permute-start | bytes 196616 | tf_op jit(solution)/shard_map/ppermute | solution.py:23
  6.6 1.9 %collective-permute-start.3 = (f32[3,2048]{1,0:T(4,128)}, f32[3,2048]{1,0:T(4,128)S(1)}, u32[]{:S(2)}, u32[]{:S(2)}) collective-permute-start(f32[3,2048]{1,0:T(4,128)} %param.11), channel_id=1, source_target_pairs={{1,0},{2,1},{3,2},{4,3},{5,4},{6,5},{7,6},{8,7},{9,8},{10,9},{11,1... | collective-permute-start | bytes 73736 | tf_op jit(solution)/shard_map/ppermute | solution.py:25
  8.5 3.6 %collective-permute-start.2 = (f32[3,2048]{1,0:T(4,128)}, f32[3,2048]{1,0:T(4,128)S(1)}, u32[]{:S(2)}, u32[]{:S(2)}) collective-permute-start(f32[3,2048]{1,0:T(4,128)} %param.11), channel_id=1, source_target_pairs={{0,1},{1,2},{2,3},{3,4},{4,5},{5,6},{6,7},{7,8},{8,9},{9,10},{10,1... | collective-permute-start | bytes 73736 | tf_op jit(solution)/shard_map/ppermute | solution.py:23
  12.2 1.0 %fusion.16 = f32[8,64,16]{1,2,0:T(8,128)S(1)} fusion(bf16[8,64,256]{2,1,0:T(8,128)(2,1)S(1)} %copy-done, bf16[2,8,8,256]{3,2,1,0:T(8,128)(2,1)} %bitcast.149), kind=kOutput, calls=%fused_computation.39 | convolution fusion | flops 4194304 | bytes 360448 | tf_op jit(solution)/shard_map/lrp,vlp->lrv/dot_general | solution.py:82
  13.2 0.0 copy-done.1
  13.2 0.2 fusion.65
  13.4 3.4 %collective-permute-start.4 = (f32[1,64,16]{1,2,0:T(8,128)S(1)}, f32[1,64,16]{1,2,0:T(8,128)S(1)}, u32[]{:S(2)}, u32[]{:S(2)}) collective-permute-start(f32[1,64,16]{1,2,0:T(8,128)S(1)} %bitcast.151), channel_id=1, source_target_pairs={{0,4},{1,5},{2,6},{3,7},{4,8},{5,9},{6,10},{7,11},{8,12},{9,13},{1... | collective-permute-start | bytes 12296 | tf_op jit(solution)/shard_map/ppermute | solution.py:35
  16.9 0.0 copy-done.5
  16.9 0.1 convolution_bitcast_fusion.1
  17.0 18.8 %all-gather.1 = f32[16,64,16]{1,2,0:T(8,128)S(1)} all-gather(f32[1,64,16]{1,2,0:T(8,128)S(1)} %convolution_bitcast_fusion.1), channel_id=2, replica_groups=mesh['parts'=2,'leaf'=16] {'leaf'}, dimensions={0}, use_global_device_ids=true | all-gather | bytes 69632 | tf_op jit(solution)/shard_map/all_gather | solution.py:90
  35.9 0.0 copy-done.7
  35.9 0.2 convolution_bitcast_fusion
  36.1 0.2 fusion.31
  36.2 0.7 fusion.64
  40.7 0.0 collective-permute-done.4
  40.7 1.3 %collective-permute-start.9 = (f32[1,64,16]{1,2,0:T(8,128)S(1)}, f32[1,64,16]{1,2,0:T(8,128)S(1)}, u32[]{:S(2)}, u32[]{:S(2)}) collective-permute-start(f32[1,64,16]{1,2,0:T(8,128)S(1)} %bitcast.152), channel_id=1, source_target_pairs={{4,0},{5,1},{6,2},{7,3},{8,4},{9,5},{10,6},{11,7},{12,8},{13,9},{1... | collective-permute-start | bytes 12296 | tf_op jit(solution)/shard_map/ppermute | solution.py:35
  42.0 0.1 convolution_add_fusion.2
  42.1 3.0 %collective-permute-done.9 = f32[1,64,16]{1,2,0:T(8,128)S(1)} collective-permute-done((f32[1,64,16]{1,2,0:T(8,128)S(1)}, f32[1,64,16]{1,2,0:T(8,128)S(1)}, u32[]{:S(2)}, u32[]{:S(2)}) %collective-permute-start.9) | collective-permute-done | bytes 4128 | tf_op jit(solution)/shard_map/ppermute | solution.py:35
  45.1 1.3 %collective-permute-start.8 = (f32[1,64,16]{1,2,0:T(8,128)S(1)}, f32[1,64,16]{1,2,0:T(8,128)S(1)}, u32[]{:S(2)}, u32[]{:S(2)}) collective-permute-start(f32[1,64,16]{1,2,0:T(8,128)S(1)} %bitcast.153), channel_id=1, source_target_pairs={{3,0},{4,1},{5,2},{6,3},{7,4},{8,5},{9,6},{10,7},{11,8},{12,9},{13... | collective-permute-start | bytes 12296 | tf_op jit(solution)/shard_map/ppermute | solution.py:35
  46.4 0.1 fusion.21
  46.5 3.6 %collective-permute-done.8 = f32[1,64,16]{1,2,0:T(8,128)S(1)} collective-permute-done((f32[1,64,16]{1,2,0:T(8,128)S(1)}, f32[1,64,16]{1,2,0:T(8,128)S(1)}, u32[]{:S(2)}, u32[]{:S(2)}) %collective-permute-start.8) | collective-permute-done | bytes 4128 | tf_op jit(solution)/shard_map/ppermute | solution.py:35
  50.0 1.3 %collective-permute-start.7 = (f32[1,64,16]{1,2,0:T(8,128)S(1)}, f32[1,64,16]{1,2,0:T(8,128)S(1)}, u32[]{:S(2)}, u32[]{:S(2)}) collective-permute-start(f32[1,64,16]{1,2,0:T(8,128)S(1)} %bitcast.154), channel_id=1, source_target_pairs={{2,0},{3,1},{4,2},{5,3},{6,4},{7,5},{8,6},{9,7},{10,8},{11,9},{12,... | collective-permute-start | bytes 12296 | tf_op jit(solution)/shard_map/ppermute | solution.py:35
  51.3 0.1 fusion.23
  51.5 3.0 %collective-permute-done.7 = f32[1,64,16]{1,2,0:T(8,128)S(1)} collective-permute-done((f32[1,64,16]{1,2,0:T(8,128)S(1)}, f32[1,64,16]{1,2,0:T(8,128)S(1)}, u32[]{:S(2)}, u32[]{:S(2)}) %collective-permute-start.7) | collective-permute-done | bytes 4128 | tf_op jit(solution)/shard_map/ppermute | solution.py:35
  54.4 3.9 %collective-permute-start.6 = (f32[1,64,16]{1,2,0:T(8,128)S(1)}, f32[1,64,16]{1,2,0:T(8,128)S(1)}, u32[]{:S(2)}, u32[]{:S(2)}) collective-permute-start(f32[1,64,16]{1,2,0:T(8,128)S(1)} %bitcast.155), channel_id=1, source_target_pairs={{0,2},{1,3},{2,4},{3,5},{4,6},{5,7},{6,8},{7,9},{8,10},{9,11},{10,... | collective-permute-start | bytes 12296 | tf_op jit(solution)/shard_map/ppermute | solution.py:35
  58.3 0.1 fusion.25
  58.4 0.7 collective-permute-done.6
  59.1 7.4 %collective-permute-start.5 = (f32[1,64,16]{1,2,0:T(8,128)S(1)}, f32[1,64,16]{1,2,0:T(8,128)S(1)}, u32[]{:S(2)}, u32[]{:S(2)}) collective-permute-start(f32[1,64,16]{1,2,0:T(8,128)S(1)} %bitcast.156), channel_id=1, source_target_pairs={{0,3},{1,4},{2,5},{3,6},{4,7},{5,8},{6,9},{7,10},{8,11},{9,12},{10... | collective-permute-start | bytes 12296 | tf_op jit(solution)/shard_map/ppermute | solution.py:35
  66.6 0.1 fusion.27
  66.7 0.7 collective-permute-done.5
  67.3 0.1 fusion.15
  67.5 0.2 fusion.10
  67.7 0.0 collective-permute-done.3
  67.7 0.0 collective-permute-done.2
  67.7 0.0 collective-permute-done.1
  67.8 0.0 collective-permute-done
  67.8 21.1 %while.10 = (s32[]{:T(128)}, f32[8,16,256]{2,1,0:T(8,128)S(1)}, s32[8,12]{1,0:T(8,128)S(1)}, bf16[16,24,256]{2,0,1:T(8,128)(2,1)S(1)}, f32[8,12]{1,0:T(8,128)S(1...) while((s32[]{:T(128)}, f32[8,16,256]{2,1,0:T(8,128)S(1)}, ...), condition=%wide.region_1.2_spmd, body=%wide.region_0.1_spmd.sunk | while | flops 33817652 | bytes 595957 | solution.py:79
  67.9 0.6 gather_fusion
  68.5 0.6 gather_fusion.1
  69.1 1.4 %fusion.83 = f32[8,16,256]{2,1,0:T(8,128)S(1)} fusion(f32[8,16,256]{2,1,0:T(8,128)S(1)} %get-tuple-element.156, s32[]{:T(128)S(6)} %copy.41, f32[12,256]{1,0:T(8,128)S(1)} %get-tuple-element.138, f32[256]{0:T(256)S(1)} %bitcast.159, f32[12,256]{1,0:T(8,128)S(1)} %get-tuple-element.140, f32[256]{0:T(256)S(1)} %bitcast.158, ...), kind=kOutput, calls=%fused_computation.5.clone.1 | convolution fusion | flops 33816576 | bytes 167428 | tf_op jit(solution)/shard_map/while/body/eval_jaxpr/npq,vnq->vp/dot_general | solution.py:77
  70.5 0.6 gather_fusion
  71.2 0.6 gather_fusion.1
  71.7 1.4 %fusion.83 = f32[8,16,256]{2,1,0:T(8,128)S(1)} fusion(f32[8,16,256]{2,1,0:T(8,128)S(1)} %get-tuple-element.156, s32[]{:T(128)S(6)} %copy.41, f32[12,256]{1,0:T(8,128)S(1)} %get-tuple-element.138, f32[256]{0:T(256)S(1)} %bitcast.159, f32[12,256]{1,0:T(8,128)S(1)} %get-tuple-element.140, f32[256]{0:T(256)S(1)} %bitcast.158, ...), kind=kOutput, calls=%fused_computation.5.clone.1 | convolution fusion | flops 33816576 | bytes 167428 | tf_op jit(solution)/shard_map/while/body/eval_jaxpr/npq,vnq->vp/dot_general | solution.py:77
  73.1 0.6 gather_fusion
  73.8 0.6 gather_fusion.1
  74.4 1.4 %fusion.83 = f32[8,16,256]{2,1,0:T(8,128)S(1)} fusion(f32[8,16,256]{2,1,0:T(8,128)S(1)} %get-tuple-element.156, s32[]{:T(128)S(6)} %copy.41, f32[12,256]{1,0:T(8,128)S(1)} %get-tuple-element.138, f32[256]{0:T(256)S(1)} %bitcast.159, f32[12,256]{1,0:T(8,128)S(1)} %get-tuple-element.140, f32[256]{0:T(256)S(1)} %bitcast.158, ...), kind=kOutput, calls=%fused_computation.5.clone.1 | convolution fusion | flops 33816576 | bytes 167428 | tf_op jit(solution)/shard_map/while/body/eval_jaxpr/npq,vnq->vp/dot_general | solution.py:77
  75.8 0.6 gather_fusion
  76.5 0.6 gather_fusion.1
  77.0 1.4 %fusion.83 = f32[8,16,256]{2,1,0:T(8,128)S(1)} fusion(f32[8,16,256]{2,1,0:T(8,128)S(1)} %get-tuple-element.156, s32[]{:T(128)S(6)} %copy.41, f32[12,256]{1,0:T(8,128)S(1)} %get-tuple-element.138, f32[256]{0:T(256)S(1)} %bitcast.159, f32[12,256]{1,0:T(8,128)S(1)} %get-tuple-element.140, f32[256]{0:T(256)S(1)} %bitcast.158, ...), kind=kOutput, calls=%fused_computation.5.clone.1 | convolution fusion | flops 33816576 | bytes 167428 | tf_op jit(solution)/shard_map/while/body/eval_jaxpr/npq,vnq->vp/dot_general | solution.py:77
  78.4 0.6 gather_fusion
  79.1 0.6 gather_fusion.1
  79.7 1.4 %fusion.83 = f32[8,16,256]{2,1,0:T(8,128)S(1)} fusion(f32[8,16,256]{2,1,0:T(8,128)S(1)} %get-tuple-element.156, s32[]{:T(128)S(6)} %copy.41, f32[12,256]{1,0:T(8,128)S(1)} %get-tuple-element.138, f32[256]{0:T(256)S(1)} %bitcast.159, f32[12,256]{1,0:T(8,128)S(1)} %get-tuple-element.140, f32[256]{0:T(256)S(1)} %bitcast.158, ...), kind=kOutput, calls=%fused_computation.5.clone.1 | convolution fusion | flops 33816576 | bytes 167428 | tf_op jit(solution)/shard_map/while/body/eval_jaxpr/npq,vnq->vp/dot_general | solution.py:77
  81.1 0.6 gather_fusion
  81.7 0.6 gather_fusion.1
  82.3 1.4 %fusion.83 = f32[8,16,256]{2,1,0:T(8,128)S(1)} fusion(f32[8,16,256]{2,1,0:T(8,128)S(1)} %get-tuple-element.156, s32[]{:T(128)S(6)} %copy.41, f32[12,256]{1,0:T(8,128)S(1)} %get-tuple-element.138, f32[256]{0:T(256)S(1)} %bitcast.159, f32[12,256]{1,0:T(8,128)S(1)} %get-tuple-element.140, f32[256]{0:T(256)S(1)} %bitcast.158, ...), kind=kOutput, calls=%fused_computation.5.clone.1 | convolution fusion | flops 33816576 | bytes 167428 | tf_op jit(solution)/shard_map/while/body/eval_jaxpr/npq,vnq->vp/dot_general | solution.py:77
  83.7 0.6 gather_fusion
  84.4 0.6 gather_fusion.1
  84.9 1.4 %fusion.83 = f32[8,16,256]{2,1,0:T(8,128)S(1)} fusion(f32[8,16,256]{2,1,0:T(8,128)S(1)} %get-tuple-element.156, s32[]{:T(128)S(6)} %copy.41, f32[12,256]{1,0:T(8,128)S(1)} %get-tuple-element.138, f32[256]{0:T(256)S(1)} %bitcast.159, f32[12,256]{1,0:T(8,128)S(1)} %get-tuple-element.140, f32[256]{0:T(256)S(1)} %bitcast.158, ...), kind=kOutput, calls=%fused_computation.5.clone.1 | convolution fusion | flops 33816576 | bytes 167428 | tf_op jit(solution)/shard_map/while/body/eval_jaxpr/npq,vnq->vp/dot_general | solution.py:77
  86.3 0.6 gather_fusion
  87.0 0.6 gather_fusion.1
  87.6 1.4 %fusion.83 = f32[8,16,256]{2,1,0:T(8,128)S(1)} fusion(f32[8,16,256]{2,1,0:T(8,128)S(1)} %get-tuple-element.156, s32[]{:T(128)S(6)} %copy.41, f32[12,256]{1,0:T(8,128)S(1)} %get-tuple-element.138, f32[256]{0:T(256)S(1)} %bitcast.159, f32[12,256]{1,0:T(8,128)S(1)} %get-tuple-element.140, f32[256]{0:T(256)S(1)} %bitcast.158, ...), kind=kOutput, calls=%fused_computation.5.clone.1 | convolution fusion | flops 33816576 | bytes 167428 | tf_op jit(solution)/shard_map/while/body/eval_jaxpr/npq,vnq->vp/dot_general | solution.py:77
  88.9 0.2 fusion.9
  89.1 0.7 copy.23
  (79 shorter events, 0.7 us)
Async XLA Ops:
  0.0 12.2 %copy-start = (bf16[8,64,256]{2,1,0:T(8,128)(2,1)S(1)}, bf16[8,64,256]{2,1,0:T(8,128)(2,1)}, u32[]{:S(2)}) copy-start(bf16[8,64,256]{2,1,0:T(8,128)(2,1)} %param.14) | copy-start | bytes 786436
  0.0 13.2 %copy-start.1 = (bf16[8,64,64]{2,1,0:T(8,128)(2,1)S(1)}, bf16[8,64,64]{2,1,0:T(8,128)(2,1)}, u32[]{:S(2)}) copy-start(bf16[8,64,64]{2,1,0:T(8,128)(2,1)} %param.15) | copy-start | bytes 196612
  0.0 67.7 %collective-permute-start.1 = (bf16[16,2048]{1,0:T(8,128)(2,1)}, bf16[16,2048]{1,0:T(8,128)(2,1)S(1)}, u32[]{:S(2)}, u32[]{:S(2)}) collective-permute-start(bf16[16,2048]{1,0:T(8,128)(2,1)} %param.12), channel_id=1, source_target_pairs={{1,0},{2,1},{3,2},{4,3},{5,4},{6,5},{7,6},{8,7},{9,8},{10,9},{11,1... | collective-permute-start | bytes 196616 | tf_op jit(solution)/shard_map/ppermute | solution.py:25
  2.1 65.7 %collective-permute-start = (bf16[16,2048]{1,0:T(8,128)(2,1)}, bf16[16,2048]{1,0:T(8,128)(2,1)S(1)}, u32[]{:S(2)}, u32[]{:S(2)}) collective-permute-start(bf16[16,2048]{1,0:T(8,128)(2,1)} %param.12), channel_id=1, source_target_pairs={{0,1},{1,2},{2,3},{3,4},{4,5},{5,6},{6,7},{7,8},{8,9},{9,10},{10,1... | collective-permute-start | bytes 196616 | tf_op jit(solution)/shard_map/ppermute | solution.py:23
  6.6 61.1 %collective-permute-start.3 = (f32[3,2048]{1,0:T(4,128)}, f32[3,2048]{1,0:T(4,128)S(1)}, u32[]{:S(2)}, u32[]{:S(2)}) collective-permute-start(f32[3,2048]{1,0:T(4,128)} %param.11), channel_id=1, source_target_pairs={{1,0},{2,1},{3,2},{4,3},{5,4},{6,5},{7,6},{8,7},{9,8},{10,9},{11,1... | collective-permute-start | bytes 73736 | tf_op jit(solution)/shard_map/ppermute | solution.py:25
  8.5 59.2 %collective-permute-start.2 = (f32[3,2048]{1,0:T(4,128)}, f32[3,2048]{1,0:T(4,128)S(1)}, u32[]{:S(2)}, u32[]{:S(2)}) collective-permute-start(f32[3,2048]{1,0:T(4,128)} %param.11), channel_id=1, source_target_pairs={{0,1},{1,2},{2,3},{3,4},{4,5},{5,6},{6,7},{7,8},{8,9},{9,10},{10,1... | collective-permute-start | bytes 73736 | tf_op jit(solution)/shard_map/ppermute | solution.py:23
  12.2 4.7 %copy-start.8 = (s32[8,12]{1,0:T(8,128)S(1)}, s32[8,12]{1,0:T(8,128)}, u32[]{:S(2)}) copy-start(s32[8,12]{1,0:T(8,128)} %param.13) | copy-start | bytes 1156
  12.2 4.7 %copy-start.5 = (bf16[1,64,64]{2,1,0:T(8,128)(2,1)S(1)}, bf16[1,64,64]{2,1,0:T(8,128)(2,1)}, u32[]{:S(2)}) copy-start(bf16[1,64,64]{2,1,0:T(8,128)(2,1)} %param.16) | copy-start | bytes 24580
  13.2 22.6 %copy-start.7 = (bf16[2,2,64,64]{3,2,1,0:T(8,128)(2,1)S(1)}, bf16[2,2,64,64]{3,2,1,0:T(8,128)(2,1)}, u32[]{:S(2)}) copy-start(bf16[2,2,64,64]{3,2,1,0:T(8,128)(2,1)} %param.19) | copy-start | bytes 98308
  13.4 22.8 %copy-start.6 = (s32[1,6]{1,0:T(1,128)S(1)}, s32[1,6]{1,0:T(1,128)}, u32[]{:S(2)}) copy-start(s32[1,6]{1,0:T(1,128)} %param.18) | copy-start | bytes 76
  13.4 28.6 %copy-start.3 = (bf16[1,6,64,64]{3,2,1,0:T(8,128)(2,1)S(1)}, bf16[1,6,64,64]{3,2,1,0:T(8,128)(2,1)}, u32[]{:S(2)}) copy-start(bf16[1,6,64,64]{3,2,1,0:T(8,128)(2,1)} %param.17) | copy-start | bytes 147460
  13.4 27.3 %collective-permute-start.4 = (f32[1,64,16]{1,2,0:T(8,128)S(1)}, f32[1,64,16]{1,2,0:T(8,128)S(1)}, u32[]{:S(2)}, u32[]{:S(2)}) collective-permute-start(f32[1,64,16]{1,2,0:T(8,128)S(1)} %bitcast.151), channel_id=1, source_target_pairs={{0,4},{1,5},{2,6},{3,7},{4,8},{5,9},{6,10},{7,11},{8,12},{9,13},{1... | collective-permute-start | bytes 12296 | tf_op jit(solution)/shard_map/ppermute | solution.py:35
  36.1 31.6 %copy-start.4 = (f32[3,2048]{1,0:T(4,128)S(1)}, f32[3,2048]{1,0:T(4,128)}, u32[]{:S(2)}) copy-start(f32[3,2048]{1,0:T(4,128)} %param.11) | copy-start | bytes 73732
  40.7 4.4 %collective-permute-start.9 = (f32[1,64,16]{1,2,0:T(8,128)S(1)}, f32[1,64,16]{1,2,0:T(8,128)S(1)}, u32[]{:S(2)}, u32[]{:S(2)}) collective-permute-start(f32[1,64,16]{1,2,0:T(8,128)S(1)} %bitcast.152), channel_id=1, source_target_pairs={{4,0},{5,1},{6,2},{7,3},{8,4},{9,5},{10,6},{11,7},{12,8},{13,9},{1... | collective-permute-start | bytes 12296 | tf_op jit(solution)/shard_map/ppermute | solution.py:35
  45.1 5.0 %collective-permute-start.8 = (f32[1,64,16]{1,2,0:T(8,128)S(1)}, f32[1,64,16]{1,2,0:T(8,128)S(1)}, u32[]{:S(2)}, u32[]{:S(2)}) collective-permute-start(f32[1,64,16]{1,2,0:T(8,128)S(1)} %bitcast.153), channel_id=1, source_target_pairs={{3,0},{4,1},{5,2},{6,3},{7,4},{8,5},{9,6},{10,7},{11,8},{12,9},{13... | collective-permute-start | bytes 12296 | tf_op jit(solution)/shard_map/ppermute | solution.py:35
  50.0 4.4 %collective-permute-start.7 = (f32[1,64,16]{1,2,0:T(8,128)S(1)}, f32[1,64,16]{1,2,0:T(8,128)S(1)}, u32[]{:S(2)}, u32[]{:S(2)}) collective-permute-start(f32[1,64,16]{1,2,0:T(8,128)S(1)} %bitcast.154), channel_id=1, source_target_pairs={{2,0},{3,1},{4,2},{5,3},{6,4},{7,5},{8,6},{9,7},{10,8},{11,9},{12,... | collective-permute-start | bytes 12296 | tf_op jit(solution)/shard_map/ppermute | solution.py:35
  51.5 16.3 %copy-start.2 = (bf16[16,2048]{1,0:T(8,128)(2,1)S(1)}, bf16[16,2048]{1,0:T(8,128)(2,1)}, u32[]{:S(2)}) copy-start(bf16[16,2048]{1,0:T(8,128)(2,1)} %param.12) | copy-start | bytes 196612
  54.4 4.7 %collective-permute-start.6 = (f32[1,64,16]{1,2,0:T(8,128)S(1)}, f32[1,64,16]{1,2,0:T(8,128)S(1)}, u32[]{:S(2)}, u32[]{:S(2)}) collective-permute-start(f32[1,64,16]{1,2,0:T(8,128)S(1)} %bitcast.155), channel_id=1, source_target_pairs={{0,2},{1,3},{2,4},{3,5},{4,6},{5,7},{6,8},{7,9},{8,10},{9,11},{10,... | collective-permute-start | bytes 12296 | tf_op jit(solution)/shard_map/ppermute | solution.py:35
  59.1 8.2 %collective-permute-start.5 = (f32[1,64,16]{1,2,0:T(8,128)S(1)}, f32[1,64,16]{1,2,0:T(8,128)S(1)}, u32[]{:S(2)}, u32[]{:S(2)}) collective-permute-start(f32[1,64,16]{1,2,0:T(8,128)S(1)} %bitcast.156), channel_id=1, source_target_pairs={{0,3},{1,4},{2,5},{3,6},{4,7},{5,8},{6,9},{7,10},{8,11},{9,12},{10... | collective-permute-start | bytes 12296 | tf_op jit(solution)/shard_map/ppermute | solution.py:35
where the time goes:
time: 90.2 us; the launch traced here: 89.8 us
  starting transfers between devices  30.7 us (34%)
  blocking collectives  18.8 us (21%)
  matrix products  13.6 us (15%)
  local copies, waits for them, and re-layouts  10.9 us (12%)
  waiting for transfers between devices  10.8 us (12%)
  between operations  4.09 us (5%)
    all_gather x1, blocking collectives, shards(): every_term = lax.all_gather(own_term[None], 'leaf', axis=0, tiled=True)  18.8 us
    ppermute x6, starting transfers between devices, passed_along(): lax.ppermute(value, axis, [(source, source + steps) for source in range(f...  18.6 us
    dot_general x8, matrix products, one_leaf(): jnp.einsum('npq,vnq->vp', kernel, source_charge, preferred_element_type=j...  10.9 us
    ppermute x6, waiting for transfers between devices, passed_along(): lax.ppermute(value, axis, [(source, source + steps) for source in range(f...  10.8 us
    ppermute x2, starting transfers between devices, padded(): lax.ppermute(tail, axis, [(i, (i + 1) % count) for i in range(ends)])  8.14 us
    gather x8, local copies, waits for them, and re-layouts, one_leaf(): source = grid_points[:, index, :]  4.66 us
    gather x8, local copies, waits for them, and re-layouts, one_leaf(): source_charge = grid_charges[:, index, :]  4.42 us
    ppermute x2, starting transfers between devices, padded(): lax.ppermute(head, axis, [((i + 1) % count, i) for i in range(ends)])  4.01 us
  transfers between devices with their start and end apart: 10, of which 5 were waited for; matrix products, arithmetic and copies ran while one was open for 4% of the time, Pallas kernels for 0%

commit v1 on v0

v1 whole, which is shorter than its diff:
```python
import functools
import math

import jax
import jax.numpy as jnp
from jax import lax
from jax.experimental import pallas as pl
from jax.experimental.pallas import tpu as pltpu
from jax.sharding import PartitionSpec as P

FAR_REACH = 4
OFFSETS = tuple(range(-FAR_REACH, -1)) + tuple(range(2, FAR_REACH + 1))
SCALE = 4.0 * math.pi
SOFT = 0.01 * SCALE * SCALE
STACK = 4
ROWS = 32
NN = (((1,), (0,)), ((), ()))
NT = (((1,), (1,)), ((), ()))
MESH = pl.DeviceIdType.MESH
f32 = jnp.float32
bf16 = jnp.bfloat16


def dot(a, b, dims):
    return lax.dot_general(a, b, dims, preferred_element_type=f32)


def fine_dot(a, b, dims):
    high = a.astype(bf16)
    low = (a - high.astype(f32)).astype(bf16)
    both = dot(jnp.concatenate([high, low], axis=0), b, dims)
    return both[: a.shape[0]] + both[a.shape[0] :]


def pieces(x):
    first = x.astype(bf16).astype(f32)
    rest = x - first
    second = rest.astype(bf16).astype(f32)
    third = (rest - second).astype(bf16).astype(f32)
    return first, second, third


def body(
    n,
    expanded,
    points,
    charges,
    near_list,
    basis,
    leaf_transfer,
    cluster_transfer,
    couple_one,
    far_list,
    couple_two,
    out,
    halo_points,
    halo_charges,
    source_charges,
    source,
    target,
    rows,
    moments,
    halo_send,
    halo_recv,
    moment_send,
    moment_recv,
):
    leaves, rank, width = basis.shape
    vectors = charges.shape[0]
    groups = couple_two.shape[0]
    group_size = n // groups
    slots = near_list.shape[1]
    me = lax.axis_index("leaf")

    barrier = pltpu.get_barrier_semaphore()

    def greet(d, carry):
        pl.semaphore_signal(
            barrier, inc=1, device_id={"leaf": lax.rem(me + d, n)}, device_id_type=MESH
        )
        return carry

    lax.fori_loop(1, n, greet, 0)

    moment_one = jnp.zeros((vectors, rank), f32)
    for k in range(leaves):
        own = charges[:, k * width : (k + 1) * width]
        source_charges[leaves + k] = own
        leaf_moment = dot(own, basis[k], NT)
        moment_one = moment_one + fine_dot(leaf_moment, leaf_transfer[k], NT)
    own_term = fine_dot(moment_one, cluster_transfer[0], NT)
    moments[me] = jnp.concatenate([moment_one, own_term], axis=1)

    pl.semaphore_wait(barrier, n - 1)

    def halo_copies(side):
        to = me + 1 if side == 0 else me - 1
        return [
            pltpu.make_async_remote_copy(
                src_ref=src,
                dst_ref=dst.at[side],
                send_sem=halo_send.at[side, m],
                recv_sem=halo_recv.at[side, m],
                device_id={"leaf": to},
                device_id_type=MESH,
            )
            for m, (src, dst) in enumerate(
                ((points, halo_points), (charges, halo_charges))
            )
        ]

    has_left, has_right = me > 0, me < n - 1

    @pl.when(has_right)
    def _():
        for copy in halo_copies(0):
            copy.start()

    @pl.when(has_left)
    def _():
        for copy in halo_copies(1):
            copy.start()

    def moment_copy(d):
        return pltpu.make_async_remote_copy(
            src_ref=moments.at[me],
            dst_ref=moments.at[me],
            send_sem=moment_send.at[d],
            recv_sem=moment_recv.at[d],
            device_id={"leaf": lax.rem(me + d, n)},
            device_id_type=MESH,
        )

    def send_moments(d, carry):
        moment_copy(d).start()
        return carry

    lax.fori_loop(1, n, send_moments, 0)

    @pl.when(jnp.logical_not(has_left))
    def _():
        halo_points[0] = jnp.zeros(halo_points.shape[1:], f32)
        halo_charges[0] = jnp.zeros(halo_charges.shape[1:], bf16)

    @pl.when(jnp.logical_not(has_right))
    def _():
        halo_points[1] = jnp.zeros(halo_points.shape[1:], f32)
        halo_charges[1] = jnp.zeros(halo_charges.shape[1:], bf16)

    own_points = points[...]
    if expanded:
        low = jnp.min(own_points, axis=1, keepdims=True)
        high = jnp.max(own_points, axis=1, keepdims=True)
        centre = (low + high) * 0.5
        rows[...] = jnp.zeros(rows.shape, f32)

        def put_rows(x, is_source):
            x = (x - centre) * SCALE
            square = jnp.sum(x * x, axis=0, keepdims=True)
            one = jnp.ones(square.shape, f32)
            if is_source:
                a, b, c = pieces(x)
                order = (a, a, a, b, b, c)
                ends = (*pieces(square), one, one, one)
            else:
                a, b, c = pieces(x * -2.0)
                order = (a, b, c, a, b, a)
                ends = (one, one, one, *pieces(square + SOFT))
            for m, block in enumerate(order):
                rows[3 * m : 3 * m + 3] = block
            for m, row in enumerate(ends):
                rows[18 + m : 19 + m] = row

        def put_sources(x, first):
            put_rows(x, True)
            for k in range(leaves):
                block = rows[:, k * width : (k + 1) * width]
                source[first + k] = jnp.transpose(block).astype(bf16)

        put_rows(own_points, False)
        for k in range(leaves):
            target[k] = rows[:, k * width : (k + 1) * width].astype(bf16)
    else:

        def put_sources(x, first):
            x = x * SCALE
            for k in range(leaves):
                source[first + k, 0:3] = x[:, k * width : (k + 1) * width]

    put_sources(own_points, leaves)

    @pl.when(has_left)
    def _():
        for copy in halo_copies(0):
            copy.wait_recv()

    @pl.when(has_right)
    def _():
        for copy in halo_copies(1):
            copy.wait_recv()

    for side in range(2):
        put_sources(halo_points[side], 2 * leaves * side)
        for k in range(leaves):
            source_charges[2 * leaves * side + k] = halo_charges[
                side, :, k * width : (k + 1) * width
            ]

    first_leaf = (me - 1) * leaves

    def one_leaf(i, carry):
        def slot_of(s):
            j = near_list[i, s]
            used = j >= 0
            j = jnp.clip(jnp.where(used, j - first_leaf, leaves), 0, 3 * leaves - 1)
            return j, source_charges[j] * used.astype(f32).astype(bf16)

        near = jnp.zeros((vectors, width), f32)
        if expanded:
            to = target[i]
            for start in range(0, slots, STACK):
                stack = [slot_of(s) for s in range(start, min(slots, start + STACK))]
                square = dot(jnp.concatenate([source[j] for j, _ in stack], axis=0), to, NN)
                kernel = lax.rsqrt(square).astype(bf16)
                near = near + dot(jnp.concatenate([c for _, c in stack], axis=1), kernel, NN)
        else:
            for c in range(3):
                row = source[leaves + i, c : c + 1, :]
                target[c] = jnp.transpose(jnp.broadcast_to(row, (128, width)))
            for s in range(slots):
                j, charge = slot_of(s)
                halves = []
                for h in range(0, width, 128):
                    square = None
                    for c in range(3):
                        gap = target[c] - source[j, c : c + 1, h : h + 128]
                        square = gap * gap + (SOFT if square is None else square)
                    halves.append(lax.rsqrt(square).astype(bf16))
                near = near + dot(charge, jnp.concatenate(halves, axis=1), NT)
        out[:, pl.ds(pl.multiple_of(i * width, width), width)] = near
        return carry

    lax.fori_loop(0, leaves, one_leaf, 0)

    def wait_moments(d, carry):
        copy = moment_copy(d)
        copy.wait_send()
        copy.wait_recv()
        return carry

    lax.fori_loop(1, n, wait_moments, 0)

    own_group = me // group_size
    local_two = jnp.zeros((vectors, rank), f32)
    for h in range(groups):
        moment_two = moments[h * group_size][:, rank:]
        for k in range(1, group_size):
            moment_two = moment_two + moments[h * group_size + k][:, rank:]
        moment_two = moment_two * jnp.where(own_group == h, 0.0, 1.0).astype(f32)
        local_two = local_two + fine_dot(moment_two, couple_two[own_group, h], NT)
    local_one = fine_dot(local_two, cluster_transfer[0], NN)
    for s, offset in enumerate(OFFSETS):
        other = me + offset
        inside = jnp.logical_and(other >= 0, other < n)
        used = jnp.logical_and(far_list[0, s] >= 0, inside).astype(f32)
        arrived = moments[jnp.where(inside, other, me)][:, :rank] * used
        local_one = local_one + fine_dot(arrived, couple_one[0, s], NT)
    for k in range(leaves):
        local_leaf = fine_dot(local_one, leaf_transfer[k], NN).astype(bf16)
        at = slice(k * width, (k + 1) * width)
        out[:, at] = out[:, at] + dot(local_leaf, basis[k], NN)

    @pl.when(has_right)
    def _():
        for copy in halo_copies(0):
            copy.wait_send()

    @pl.when(has_left)
    def _():
        for copy in halo_copies(1):
            copy.wait_send()


def shards(
    points,
    charges,
    near_list,
    basis,
    leaf_transfer,
    cluster_transfer,
    couple_one,
    far_list,
    couple_two,
):
    n = lax.axis_size("leaf")
    leaves, rank, width = basis.shape
    vectors, panels = charges.shape
    expanded = n + 2 <= 18
    source = (3 * leaves, width, ROWS) if expanded else (3 * leaves, 8, width)
    target = (leaves, ROWS, width) if expanded else (3, width, 128)
    kind = bf16 if expanded else f32
    vmem = pl.BlockSpec(memory_space=pltpu.VMEM)
    smem = pl.BlockSpec(memory_space=pltpu.SMEM)
    return pl.pallas_call(
        functools.partial(body, n, expanded),
        out_shape=jax.ShapeDtypeStruct((vectors, panels), f32),
        in_specs=[vmem, vmem, smem, vmem, vmem, vmem, vmem, smem, vmem],
        out_specs=vmem,
        scratch_shapes=[
            pltpu.VMEM((2, *points.shape), f32),
            pltpu.VMEM((2, vectors, panels), bf16),
            pltpu.VMEM((3 * leaves, vectors, width), bf16),
            pltpu.VMEM(source, kind),
            pltpu.VMEM(target, kind),
            pltpu.VMEM((ROWS, panels), f32),
            pltpu.VMEM((n, vectors, 2 * rank), f32),
            pltpu.SemaphoreType.DMA((2, 2)),
            pltpu.SemaphoreType.DMA((2, 2)),
            pltpu.SemaphoreType.DMA((n,)),
            pltpu.SemaphoreType.DMA((n,)),
        ],
        compiler_params=pltpu.CompilerParams(
            collective_id=0, has_side_effects=True, vmem_limit_bytes=40 << 20
        ),
        name="product",
    )(
        points,
        charges,
        near_list,
        basis,
        leaf_transfer,
        cluster_transfer,
        couple_one,
        far_list,
        couple_two,
    )


def solution(mesh):
    return jax.shard_map(
        shards,
        mesh=mesh,
        in_specs=(
            P(None, ("parts", "leaf")),
            P(None, ("parts", "leaf")),
            P(("parts", "leaf"), None),
            P(("parts", "leaf"), None, None),
            P(("parts", "leaf"), None, None),
            P(("parts", "leaf"), None, None),
            P(("parts", "leaf"), None, None, None),
            P(("parts", "leaf"), None),
            P("parts", None, None, None),
        ),
        out_specs=P(None, ("parts", "leaf")),
        check_vma=False,
    )
```

time: 90.2 us -> 27 us (0.30)
  starting transfers between devices: 30.7 us -> 0 us
  blocking collectives: 18.8 us -> 0 us
  Pallas kernels: 0 us -> 18.6 us
  matrix products: 13.6 us -> 0 us
  waiting for transfers between devices: 10.8 us -> 0 us
  between operations: 4.09 us -> 0.02 us
  local copies, waits for them, and re-layouts: 10.9 us -> 7.9 us
    ppermute x10 -> x0, starting transfers between devices: 30.7 us -> none  [the longest x6 18.6 us: passed_along(): lax.ppermute(value, axis, [(source, source + steps) for source in range(f...]
    all_gather x1 -> x0, blocking collectives: 18.8 us -> none  [shards(): every_term = lax.all_gather(own_term[None], 'leaf', axis=0, tiled=True)]
    pallas_call x0 -> x1, Pallas kernels: none -> 18.6 us  [shards(): pl.pallas_call(functools.partial(body, n, expanded), out_shape=jax.ShapeD...]
    dot_general x21 -> x0, matrix products: 13.6 us -> none  [the longest x8 10.9 us: one_leaf(): jnp.einsum('npq,vnq->vp', kernel, source_charge, preferred_element_type=j...]
    ppermute x10 -> x0, waiting for transfers between devices: 10.8 us -> none  [the longest x6 10.8 us: passed_along(): lax.ppermute(value, axis, [(source, source + steps) for source in range(f...]
    gather x16 -> x0, local copies, waits for them, and re-layouts: 9.08 us -> none  [the longest x8 4.66 us: one_leaf(): source = grid_points[:, index, :]]
    unnamed x18 -> x19, local copies, waits for them, and re-layouts: 0.03 us -> 7.9 us
    slice x17 -> x0, local copies, waits for them, and re-layouts: 1.03 us -> none  [the longest x1 0.69 us: shards(): valid = (far_list[0, slot] >= 0).astype(jnp.float32)]
  transfers between devices with their start and end apart: 10 -> 0, of which waited for: 5 -> 0; matrix products, arithmetic and copies ran while one was open for 4% -> 0% of each run, Pallas kernels for 0% -> 0%
where the time goes in v1:
time: 27 us; the launch traced here: 26.5 us
  Pallas kernels  18.6 us (69%)
  local copies, waits for them, and re-layouts  7.9 us (29%)
    pallas_call x1, Pallas kernels, shards(): pl.pallas_call(functools.partial(body, n, expanded), out_shape=jax.ShapeD...  18.6 us
    unnamed x19, local copies, waits for them, and re-layouts  7.9 us

profile of v1, /device:TPU:1, one launch (start us, length us, event | category | flops | bytes accessed | tf_op | source)
XLA Modules:
  0.0 26.5 jit_solution(4890045595804098834)
XLA Ops:
  0.0 0.0 copy-start
  0.0 0.9 %copy-done = bf16[8,64,256]{2,1,0:T(8,128)(2,1)S(1)} copy-done((bf16[8,64,256]{2,1,0:T(8,128)(2,1)S(1)}, bf16[8,64,256]{2,1,0:T(8,128)(2,1)}, u32[]{:S(2)}) %copy-start) | copy-done | bytes 262168
  1.0 0.0 copy-start.1
  1.0 0.9 %copy-done.1 = bf16[8,64,64]{2,1,0:T(8,128)(2,1)S(1)} copy-done((bf16[8,64,64]{2,1,0:T(8,128)(2,1)S(1)}, bf16[8,64,64]{2,1,0:T(8,128)(2,1)}, u32[]{:S(2)}) %copy-start.1) | copy-done | bytes 65560
  1.9 0.0 copy-start.2
  1.9 0.9 %copy-done.2 = bf16[1,6,64,64]{3,2,1,0:T(8,128)(2,1)S(1)} copy-done((bf16[1,6,64,64]{3,2,1,0:T(8,128)(2,1)S(1)}, bf16[1,6,64,64]{3,2,1,0:T(8,128)(2,1)}, u32[]{:S(2)}) %copy-start.2) | copy-done | bytes 49176
  2.7 0.0 copy-start.3
  2.8 0.8 %copy-done.3 = bf16[16,2048]{1,0:T(8,128)(2,1)S(1)} copy-done((bf16[16,2048]{1,0:T(8,128)(2,1)S(1)}, bf16[16,2048]{1,0:T(8,128)(2,1)}, u32[]{:S(2)}) %copy-start.3) | copy-done | bytes 65560
  3.6 0.0 copy-start.4
  3.6 0.8 %copy-done.4 = bf16[2,2,64,64]{3,2,1,0:T(8,128)(2,1)S(1)} copy-done((bf16[2,2,64,64]{3,2,1,0:T(8,128)(2,1)S(1)}, bf16[2,2,64,64]{3,2,1,0:T(8,128)(2,1)}, u32[]{:S(2)}) %copy-start.4) | copy-done | bytes 32792
  4.4 0.0 copy-start.5
  4.4 0.8 %copy-done.5 = f32[3,2048]{1,0:T(4,128)S(1)} copy-done((f32[3,2048]{1,0:T(4,128)S(1)}, f32[3,2048]{1,0:T(4,128)}, u32[]{:S(2)}) %copy-start.5) | copy-done | bytes 24600
  5.2 0.0 copy-start.6
  5.2 0.7 %copy-done.6 = bf16[1,64,64]{2,1,0:T(8,128)(2,1)S(1)} copy-done((bf16[1,64,64]{2,1,0:T(8,128)(2,1)S(1)}, bf16[1,64,64]{2,1,0:T(8,128)(2,1)}, u32[]{:S(2)}) %copy-start.6) | copy-done | bytes 8216
  5.9 0.0 copy-start.7
  5.9 0.7 %copy-done.7 = s32[8,12]{1,0:T(8,128)S(1)} copy-done((s32[8,12]{1,0:T(8,128)S(1)}, s32[8,12]{1,0:T(8,128)}, u32[]{:S(2)}) %copy-start.7) | copy-done | bytes 408
  6.6 0.0 copy-start.8
  6.6 0.7 %copy-done.8 = s32[1,6]{1,0:T(1,128)S(1)} copy-done((s32[1,6]{1,0:T(1,128)S(1)}, s32[1,6]{1,0:T(1,128)}, u32[]{:S(2)}) %copy-start.8) | copy-done | bytes 48
  7.2 18.6 %product.1 = f32[16,2048]{1,0:T(8,128)S(1)} custom-call(f32[3,2048]{1,0:T(4,128)S(1)} %copy-done.5, bf16[16,2048]{1,0:T(8,128)(2,1)S(1)} %copy-done.3, s32[8,12]{1,0:T(8,128)S(1)} %copy-done.7, bf16[8,64,256]{2,1,0:T(8,128)(2,1)S(1)} %copy-done, bf16[8,64,64]{2,1,0:T(8,128)(2,1)S(1)} %copy-done.1, bf16[1,64,64]{2,1,0:T(8,128)(2,1)S(1)} %copy-done.6, ...), custom_call_target="tpu_custom_call" | custom-call | tf_op jit(solution)/shard_map/product/pallas_call | solution.py:304
  25.9 0.7 %copy.11 = f32[16,2048]{1,0:T(8,128)} copy(f32[16,2048]{1,0:T(8,128)S(1)} %product.1) | data formatting | bytes 262144
Async XLA Ops:
  0.0 0.9 %copy-start = (bf16[8,64,256]{2,1,0:T(8,128)(2,1)S(1)}, bf16[8,64,256]{2,1,0:T(8,128)(2,1)}, u32[]{:S(2)}) copy-start(bf16[8,64,256]{2,1,0:T(8,128)(2,1)} %basis.1) | copy-start | bytes 786436
  1.0 0.9 %copy-start.1 = (bf16[8,64,64]{2,1,0:T(8,128)(2,1)S(1)}, bf16[8,64,64]{2,1,0:T(8,128)(2,1)}, u32[]{:S(2)}) copy-start(bf16[8,64,64]{2,1,0:T(8,128)(2,1)} %leaf_transfer.1) | copy-start | bytes 196612
  1.9 0.9 %copy-start.2 = (bf16[1,6,64,64]{3,2,1,0:T(8,128)(2,1)S(1)}, bf16[1,6,64,64]{3,2,1,0:T(8,128)(2,1)}, u32[]{:S(2)}) copy-start(bf16[1,6,64,64]{3,2,1,0:T(8,128)(2,1)} %couple_one.1) | copy-start | bytes 147460
  2.7 0.8 %copy-start.3 = (bf16[16,2048]{1,0:T(8,128)(2,1)S(1)}, bf16[16,2048]{1,0:T(8,128)(2,1)}, u32[]{:S(2)}) copy-start(bf16[16,2048]{1,0:T(8,128)(2,1)} %charges.1) | copy-start | bytes 196612
  3.6 0.8 %copy-start.4 = (bf16[2,2,64,64]{3,2,1,0:T(8,128)(2,1)S(1)}, bf16[2,2,64,64]{3,2,1,0:T(8,128)(2,1)}, u32[]{:S(2)}) copy-start(bf16[2,2,64,64]{3,2,1,0:T(8,128)(2,1)} %couple_two.1) | copy-start | bytes 98308
  4.4 0.8 %copy-start.5 = (f32[3,2048]{1,0:T(4,128)S(1)}, f32[3,2048]{1,0:T(4,128)}, u32[]{:S(2)}) copy-start(f32[3,2048]{1,0:T(4,128)} %points.1) | copy-start | bytes 73732
  5.2 0.7 %copy-start.6 = (bf16[1,64,64]{2,1,0:T(8,128)(2,1)S(1)}, bf16[1,64,64]{2,1,0:T(8,128)(2,1)}, u32[]{:S(2)}) copy-start(bf16[1,64,64]{2,1,0:T(8,128)(2,1)} %cluster_transfer.1) | copy-start | bytes 24580
  5.9 0.7 %copy-start.7 = (s32[8,12]{1,0:T(8,128)S(1)}, s32[8,12]{1,0:T(8,128)}, u32[]{:S(2)}) copy-start(s32[8,12]{1,0:T(8,128)} %near_list.1) | copy-start | bytes 1156
  6.6 0.7 %copy-start.8 = (s32[1,6]{1,0:T(1,128)S(1)}, s32[1,6]{1,0:T(1,128)}, u32[]{:S(2)}) copy-start(s32[1,6]{1,0:T(1,128)} %far_list.1) | copy-start | bytes 76

commit v2 on v1

--- a/solution.py
+++ b/solution.py
@@ -43,6 +43,16 @@
 def body(
     n,
     expanded,
+    points_in,
+    charges_in,
+    near_list_in,
+    basis_in,
+    leaf_transfer_in,
+    cluster_transfer_in,
+    couple_one_in,
+    far_list_in,
+    couple_two_in,
+    out,
     points,
     charges,
     near_list,
@@ -52,7 +62,7 @@
     couple_one,
     far_list,
     couple_two,
-    out,
+    input_sem,
     halo_points,
     halo_charges,
     source_charges,
@@ -69,8 +79,28 @@
     vectors = charges.shape[0]
     groups = couple_two.shape[0]
     group_size = n // groups
+    own_group = lax.axis_index("leaf") // group_size
     slots = near_list.shape[1]
     me = lax.axis_index("leaf")
+
+    inputs = [
+        pltpu.make_async_copy(src, dst, input_sem.at[m])
+        for m, (src, dst) in enumerate(
+            (
+                (charges_in, charges),
+                (basis_in, basis),
+                (leaf_transfer_in, leaf_transfer),
+                (points_in, points),
+                (near_list_in, near_list),
+                (cluster_transfer_in, cluster_transfer),
+                (couple_one_in, couple_one),
+                (far_list_in, far_list),
+                (couple_two_in.at[own_group], couple_two),
+            )
+        )
+    ]
+    for copy in inputs:
+        copy.start()
 
     barrier = pltpu.get_barrier_semaphore()
 
@@ -81,6 +111,9 @@
         return carry
 
     lax.fori_loop(1, n, greet, 0)
+
+    for copy in inputs:
+        copy.wait()
 
     moment_one = jnp.zeros((vectors, rank), f32)
     for k in range(leaves):
@@ -105,7 +138,7 @@
                 device_id_type=MESH,
             )
             for m, (src, dst) in enumerate(
-                ((points, halo_points), (charges, halo_charges))
+                ((points_in, halo_points), (charges_in, halo_charges))
             )
         ]
 
@@ -250,14 +283,13 @@
 
     lax.fori_loop(1, n, wait_moments, 0)
 
-    own_group = me // group_size
     local_two = jnp.zeros((vectors, rank), f32)
     for h in range(groups):
         moment_two = moments[h * group_size][:, rank:]
         for k in range(1, group_size):
             moment_two = moment_two + moments[h * group_size + k][:, rank:]
         moment_two = moment_two * jnp.where(own_group == h, 0.0, 1.0).astype(f32)
-        local_two = local_two + fine_dot(moment_two, couple_two[own_group, h], NT)
+        local_two = local_two + fine_dot(moment_two, couple_two[h], NT)
     local_one = fine_dot(local_two, cluster_transfer[0], NN)
     for s, offset in enumerate(OFFSETS):
         other = me + offset
@@ -299,14 +331,24 @@
     source = (3 * leaves, width, ROWS) if expanded else (3 * leaves, 8, width)
     target = (leaves, ROWS, width) if expanded else (3, width, 128)
     kind = bf16 if expanded else f32
+    hbm = pl.BlockSpec(memory_space=pltpu.HBM)
     vmem = pl.BlockSpec(memory_space=pltpu.VMEM)
-    smem = pl.BlockSpec(memory_space=pltpu.SMEM)
     return pl.pallas_call(
         functools.partial(body, n, expanded),
         out_shape=jax.ShapeDtypeStruct((vectors, panels), f32),
-        in_specs=[vmem, vmem, smem, vmem, vmem, vmem, vmem, smem, vmem],
+        in_specs=[hbm] * 9,
         out_specs=vmem,
         scratch_shapes=[
+            pltpu.VMEM(points.shape, f32),
+            pltpu.VMEM(charges.shape, bf16),
+            pltpu.SMEM(near_list.shape, jnp.int32),
+            pltpu.VMEM(basis.shape, bf16),
+            pltpu.VMEM(leaf_transfer.shape, bf16),
+            pltpu.VMEM(cluster_transfer.shape, bf16),
+            pltpu.VMEM(couple_one.shape, bf16),
+            pltpu.SMEM(far_list.shape, jnp.int32),
+            pltpu.VMEM(couple_two.shape[1:], bf16),
+            pltpu.SemaphoreType.DMA((9,)),
             pltpu.VMEM((2, *points.shape), f32),
             pltpu.VMEM((2, vectors, panels), bf16),
             pltpu.VMEM((3 * leaves, vectors, width), bf16),
@@ -320,7 +362,7 @@
             pltpu.SemaphoreType.DMA((n,)),
         ],
         compiler_params=pltpu.CompilerParams(
-            collective_id=0, has_side_effects=True, vmem_limit_bytes=40 << 20
+            collective_id=0, has_side_effects=True, vmem_limit_bytes=62 << 20
         ),
         name="product",
     )(

time: 27 us -> 20.6 us (0.76); the launches traced: 26.5 us -> 20.4 us
  local copies, waits for them, and re-layouts: 7.9 us -> 1.57 us
  Pallas kernels: 18.6 us -> 18.9 us
    unnamed x19 -> x1, local copies, waits for them, and re-layouts: 7.9 us -> 1.57 us
where the time goes in v2:
time: 20.6 us; the launch traced here: 20.4 us
  Pallas kernels  18.9 us (92%)
  local copies, waits for them, and re-layouts  1.57 us (8%)
    pallas_call x1, Pallas kernels, shards(): pl.pallas_call(functools.partial(body, n, expanded), out_shape=jax.ShapeD...  18.9 us
    unnamed x1, local copies, waits for them, and re-layouts  1.57 us

profile of v2, /device:TPU:1, one launch (start us, length us, event | category | flops | bytes accessed | tf_op | source)
XLA Modules:
  0.0 20.4 jit_solution(2689784908517238592)
XLA Ops:
  0.0 18.9 %product.1 = f32[16,2048]{1,0:T(8,128)} custom-call(f32[3,2048]{1,0:T(4,128)} %points_in.1, bf16[16,2048]{1,0:T(8,128)(2,1)} %charges_in.1, s32[8,12]{1,0:T(8,128)} %near_list_in.1, bf16[8,64,256]{2,1,0:T(8,128)(2,1)} %basis_in.1, bf16[8,64,64]{2,1,0:T(8,128)(2,1)} %leaf_transfer_in.1, bf16[1,64,64]{2,1,0:T(8,128)(2,1)} %cluster_transfer_in.1, ...), custom_call_target="tpu_custom_call" | custom-call | tf_op jit(solution)/shard_map/product/pallas_call | solution.py:336
  18.9 1.6 %copy.11 = f32[16,2048]{1,0:T(8,128)} copy(f32[16,2048]{1,0:T(8,128)} %product.1) | data formatting | bytes 262144

commit v3 on v2

--- a/solution.py
+++ b/solution.py
@@ -335,7 +335,7 @@
     vmem = pl.BlockSpec(memory_space=pltpu.VMEM)
     return pl.pallas_call(
         functools.partial(body, n, expanded),
-        out_shape=jax.ShapeDtypeStruct((vectors, panels), f32),
+        out_shape=pltpu.VMEM((vectors, panels), f32),
         in_specs=[hbm] * 9,
         out_specs=vmem,
         scratch_shapes=[

time: 20.6 us -> 19 us (0.922)
  local copies, waits for them, and re-layouts: 1.57 us -> 0.66 us
  Pallas kernels: 18.9 us -> 18.2 us
    unnamed x1, local copies, waits for them, and re-layouts: 1.57 us -> 0.66 us
    pallas_call x1, Pallas kernels: 18.9 us -> 18.2 us  [shards(): pl.pallas_call(functools.partial(body, n, expanded), out_shape=pltpu.VMEM...]
where the time goes in v3:
time: 19 us; the launch traced here: 18.9 us
  Pallas kernels  18.2 us (96%)
  local copies, waits for them, and re-layouts  0.66 us (3%)
    pallas_call x1, Pallas kernels, shards(): pl.pallas_call(functools.partial(body, n, expanded), out_shape=pltpu.VMEM...  18.2 us
    unnamed x1, local copies, waits for them, and re-layouts  0.66 us

profile of v3, /device:TPU:1, one launch (start us, length us, event | category | flops | bytes accessed | tf_op | source)
XLA Modules:
  0.0 18.9 jit_solution(18121933561489315779)
XLA Ops:
  0.0 18.2 %product.1 = f32[16,2048]{1,0:T(8,128)S(1)} custom-call(f32[3,2048]{1,0:T(4,128)} %points_in.1, bf16[16,2048]{1,0:T(8,128)(2,1)} %charges_in.1, s32[8,12]{1,0:T(8,128)} %near_list_in.1, bf16[8,64,256]{2,1,0:T(8,128)(2,1)} %basis_in.1, bf16[8,64,64]{2,1,0:T(8,128)(2,1)} %leaf_transfer_in.1, bf16[1,64,64]{2,1,0:T(8,128)(2,1)} %cluster_transfer_in.1, ...), custom_call_target="tpu_custom_call" | custom-call | tf_op jit(solution)/shard_map/product/pallas_call | solution.py:336
  18.2 0.7 %copy.11 = f32[16,2048]{1,0:T(8,128)} copy(f32[16,2048]{1,0:T(8,128)S(1)} %product.1) | data formatting | bytes 262144

commit v4 on v3

--- a/solution.py
+++ b/solution.py
@@ -14,6 +14,8 @@
 SOFT = 0.01 * SCALE * SCALE
 STACK = 4
 ROWS = 32
+UNROLL = 5
+LAST = 4
 NN = (((1,), (0,)), ((), ()))
 NT = (((1,), (1,)), ((), ()))
 MESH = pl.DeviceIdType.MESH
@@ -74,6 +76,7 @@
     halo_recv,
     moment_send,
     moment_recv,
+    news,
 ):
     leaves, rank, width = basis.shape
     vectors = charges.shape[0]
@@ -83,6 +86,37 @@
     slots = near_list.shape[1]
     me = lax.axis_index("leaf")
 
+    barrier = pltpu.get_barrier_semaphore()
+
+    has_left, has_right = me > 0, me < n - 1
+
+    def on_line(step, act_left, act_right):
+        pl.when(me >= step)(functools.partial(act_left, {"leaf": me - step}))
+        pl.when(me < n - step)(functools.partial(act_right, {"leaf": me + step}))
+
+    def greet(device):
+        pl.semaphore_signal(barrier, inc=1, device_id=device, device_id_type=MESH)
+
+    on_line(1, greet, greet)
+
+    rounds = max(1, (n - 2).bit_length())
+
+    def announce(r):
+        def to(side):
+            return lambda device: pl.semaphore_signal(
+                news.at[r, side], inc=1, device_id=device, device_id_type=MESH
+            )
+
+        on_line(2**r, to(1), to(0))
+
+    def hear(r):
+        def of(side):
+            return lambda device: pl.semaphore_wait(news.at[r, side], 1)
+
+        on_line(2**r, of(0), of(1))
+        if r + 1 < rounds:
+            announce(r + 1)
+
     inputs = [
         pltpu.make_async_copy(src, dst, input_sem.at[m])
         for m, (src, dst) in enumerate(
@@ -90,9 +124,9 @@
                 (charges_in, charges),
                 (basis_in, basis),
                 (leaf_transfer_in, leaf_transfer),
+                (cluster_transfer_in, cluster_transfer),
                 (points_in, points),
                 (near_list_in, near_list),
-                (cluster_transfer_in, cluster_transfer),
                 (couple_one_in, couple_one),
                 (far_list_in, far_list),
                 (couple_two_in.at[own_group], couple_two),
@@ -102,29 +136,8 @@
     for copy in inputs:
         copy.start()
 
-    barrier = pltpu.get_barrier_semaphore()
-
-    def greet(d, carry):
-        pl.semaphore_signal(
-            barrier, inc=1, device_id={"leaf": lax.rem(me + d, n)}, device_id_type=MESH
-        )
-        return carry
-
-    lax.fori_loop(1, n, greet, 0)
-
-    for copy in inputs:
-        copy.wait()
-
-    moment_one = jnp.zeros((vectors, rank), f32)
-    for k in range(leaves):
-        own = charges[:, k * width : (k + 1) * width]
-        source_charges[leaves + k] = own
-        leaf_moment = dot(own, basis[k], NT)
-        moment_one = moment_one + fine_dot(leaf_moment, leaf_transfer[k], NT)
-    own_term = fine_dot(moment_one, cluster_transfer[0], NT)
-    moments[me] = jnp.concatenate([moment_one, own_term], axis=1)
-
-    pl.semaphore_wait(barrier, n - 1)
+    pl.semaphore_wait(barrier, has_left.astype(jnp.int32) + has_right.astype(jnp.int32))
+    announce(0)
 
     def halo_copies(side):
         to = me + 1 if side == 0 else me - 1
@@ -142,8 +155,6 @@
             )
         ]
 
-    has_left, has_right = me > 0, me < n - 1
-
     @pl.when(has_right)
     def _():
         for copy in halo_copies(0):
@@ -153,13 +164,25 @@
     def _():
         for copy in halo_copies(1):
             copy.start()
+
+    for copy in inputs[:4]:
+        copy.wait()
+
+    moment_one = jnp.zeros((vectors, rank), f32)
+    for k in range(leaves):
+        own = charges[:, k * width : (k + 1) * width]
+        source_charges[leaves + k] = own
+        leaf_moment = dot(own, basis[k], NT)
+        moment_one = moment_one + fine_dot(leaf_moment, leaf_transfer[k], NT)
+    own_term = fine_dot(moment_one, cluster_transfer[0], NT)
+    moments[me] = jnp.concatenate([moment_one, own_term], axis=1)
 
     def moment_copy(d):
         return pltpu.make_async_remote_copy(
             src_ref=moments.at[me],
             dst_ref=moments.at[me],
-            send_sem=moment_send.at[d],
-            recv_sem=moment_recv.at[d],
+            send_sem=moment_send,
+            recv_sem=moment_recv,
             device_id={"leaf": lax.rem(me + d, n)},
             device_id_type=MESH,
         )
@@ -168,7 +191,6 @@
         moment_copy(d).start()
         return carry
 
-    lax.fori_loop(1, n, send_moments, 0)
 
     @pl.when(jnp.logical_not(has_left))
     def _():
@@ -180,6 +202,7 @@
         halo_points[1] = jnp.zeros(halo_points.shape[1:], f32)
         halo_charges[1] = jnp.zeros(halo_charges.shape[1:], bf16)
 
+    inputs[4].wait()
     own_points = points[...]
     if expanded:
         low = jnp.min(own_points, axis=1, keepdims=True)
@@ -239,6 +262,8 @@
                 side, :, k * width : (k + 1) * width
             ]
 
+    for copy in inputs[5:]:
+        copy.wait()
     first_leaf = (me - 1) * leaves
 
     def one_leaf(i, carry):
@@ -273,15 +298,18 @@
         out[:, pl.ds(pl.multiple_of(i * width, width), width)] = near
         return carry
 
-    lax.fori_loop(0, leaves, one_leaf, 0)
-
-    def wait_moments(d, carry):
-        copy = moment_copy(d)
-        copy.wait_send()
-        copy.wait_recv()
-        return carry
-
-    lax.fori_loop(1, n, wait_moments, 0)
+    done = 0
+    for r in range(rounds):
+        upto = r * (leaves - LAST) // max(1, rounds - 1)
+        if upto > done:
+            lax.fori_loop(done, upto, one_leaf, 0)
+        done = upto
+        hear(r)
+    lax.fori_loop(1, n, send_moments, 0, unroll=UNROLL)
+    lax.fori_loop(done, leaves, one_leaf, 0)
+
+    others = moments.at[pl.ds(0, n - 1)]
+    pltpu.make_async_copy(others, others, moment_recv).wait()
 
     local_two = jnp.zeros((vectors, rank), f32)
     for h in range(groups):
@@ -301,6 +329,8 @@
         local_leaf = fine_dot(local_one, leaf_transfer[k], NN).astype(bf16)
         at = slice(k * width, (k + 1) * width)
         out[:, at] = out[:, at] + dot(local_leaf, basis[k], NN)
+
+    pltpu.make_async_copy(others, others, moment_send).wait()
 
     @pl.when(has_right)
     def _():
@@ -358,8 +388,9 @@
             pltpu.VMEM((n, vectors, 2 * rank), f32),
             pltpu.SemaphoreType.DMA((2, 2)),
             pltpu.SemaphoreType.DMA((2, 2)),
-            pltpu.SemaphoreType.DMA((n,)),
-            pltpu.SemaphoreType.DMA((n,)),
+            pltpu.SemaphoreType.DMA,
+            pltpu.SemaphoreType.DMA,
+            pltpu.SemaphoreType.REGULAR(((n - 1).bit_length(), 2)),
         ],
         compiler_params=pltpu.CompilerParams(
             collective_id=0, has_side_effects=True, vmem_limit_bytes=62 << 20

time: 19 us -> 18.8 us (0.989)
  the two profiles are of different devices: /device:TPU:1 before, /device:TPU:0 now
where the time goes in v4:
time: 18.8 us; the launch traced here: 18.7 us
  Pallas kernels  18 us (96%)
  local copies, waits for them, and re-layouts  0.66 us (4%)
    pallas_call x1, Pallas kernels, shards(): pl.pallas_call(functools.partial(body, n, expanded), out_shape=pltpu.VMEM...  18 us
    unnamed x1, local copies, waits for them, and re-layouts  0.66 us

profile of v4, /device:TPU:0, one launch (start us, length us, event | category | flops | bytes accessed | tf_op | source)
XLA Modules:
  0.0 18.7 jit_solution(8375151457848547381)
XLA Ops:
  0.0 18.0 %product.1 = f32[16,2048]{1,0:T(8,128)S(1)} custom-call(f32[3,2048]{1,0:T(4,128)} %points_in.1, bf16[16,2048]{1,0:T(8,128)(2,1)} %charges_in.1, s32[8,12]{1,0:T(8,128)} %near_list_in.1, bf16[8,64,256]{2,1,0:T(8,128)(2,1)} %basis_in.1, bf16[8,64,64]{2,1,0:T(8,128)(2,1)} %leaf_transfer_in.1, bf16[1,64,64]{2,1,0:T(8,128)(2,1)} %cluster_transfer_in.1, ...), custom_call_target="tpu_custom_call" | custom-call | tf_op jit(solution)/shard_map/product/pallas_call | solution.py:366
  18.0 0.7 %copy.11 = f32[16,2048]{1,0:T(8,128)} copy(f32[16,2048]{1,0:T(8,128)S(1)} %product.1) | data formatting | bytes 262144

commit v5 on v4

--- a/solution.py
+++ b/solution.py
@@ -302,11 +302,11 @@
     for r in range(rounds):
         upto = r * (leaves - LAST) // max(1, rounds - 1)
         if upto > done:
-            lax.fori_loop(done, upto, one_leaf, 0)
+            lax.fori_loop(done, upto, one_leaf, 0, unroll=min(2, upto - done))
         done = upto
         hear(r)
     lax.fori_loop(1, n, send_moments, 0, unroll=UNROLL)
-    lax.fori_loop(done, leaves, one_leaf, 0)
+    lax.fori_loop(done, leaves, one_leaf, 0, unroll=2)
 
     others = moments.at[pl.ds(0, n - 1)]
     pltpu.make_async_copy(others, others, moment_recv).wait()

time: 18.8 us -> 18.6 us (0.989)
  Pallas kernels: 18 us -> 17.8 us
    pallas_call x1, Pallas kernels: 18 us -> 17.8 us  [shards(): pl.pallas_call(functools.partial(body, n, expanded), out_shape=pltpu.VMEM...]
where the time goes in v5:
time: 18.6 us; the launch traced here: 18.4 us
  Pallas kernels  17.8 us (96%)
  local copies, waits for them, and re-layouts  0.66 us (4%)
    pallas_call x1, Pallas kernels, shards(): pl.pallas_call(functools.partial(body, n, expanded), out_shape=pltpu.VMEM...  17.8 us
    unnamed x1, local copies, waits for them, and re-layouts  0.66 us

profile of v5, /device:TPU:0, one launch (start us, length us, event | category | flops | bytes accessed | tf_op | source)
XLA Modules:
  0.0 18.4 jit_solution(4585529179683700576)
XLA Ops:
  0.0 17.8 %product.1 = f32[16,2048]{1,0:T(8,128)S(1)} custom-call(f32[3,2048]{1,0:T(4,128)} %points_in.1, bf16[16,2048]{1,0:T(8,128)(2,1)} %charges_in.1, s32[8,12]{1,0:T(8,128)} %near_list_in.1, bf16[8,64,256]{2,1,0:T(8,128)(2,1)} %basis_in.1, bf16[8,64,64]{2,1,0:T(8,128)(2,1)} %leaf_transfer_in.1, bf16[1,64,64]{2,1,0:T(8,128)(2,1)} %cluster_transfer_in.1, ...), custom_call_target="tpu_custom_call" | custom-call | tf_op jit(solution)/shard_map/product/pallas_call | solution.py:366
  17.8 0.7 %copy.11 = f32[16,2048]{1,0:T(8,128)} copy(f32[16,2048]{1,0:T(8,128)S(1)} %product.1) | data formatting | bytes 262144
